TPU v7x, 256 devices: a whole 4x4x8 slice. The times are simulated.
256 devices in a mesh: phase: 8 (over x, core), seq: 16 (over y_lo, z), mp: 2 (over y_hi).
Axes of the slice: x: 4, y: 4 (y_hi: 2, y_lo: 2; y = y_hi * 2 + y_lo), z: 8, core: 2. Of those that a mesh axis runs over, the one named last changes fastest.
Arguments:
- queries: bfloat16 [8, 8192, 4096], P('phase', 'seq', 'mp'), may hold values from -360 to 360
- key_weight: bfloat16 [8, 1024, 4096], P('phase', None, 'mp'), may hold values from -0.1875 to 0.1875
- value_weight: bfloat16 [8, 1024, 4096], P('phase', None, 'mp'), may hold values from -0.1875 to 0.1875
- enc_gain: float32 [1024], replicated, may hold values from 0.25 to 2
- neighbour_states: bfloat16 [512, 64, 1024], P('seq', ('phase', 'mp')), may hold values from -600 to 600
- slot_dest: int32 [512], P('seq'), may hold values from -1 to 255, as said below
Outputs:
- context: bfloat16 [8, 8192, 4096], P('phase', 'seq', 'mp')
Inputs may be any that keep to these rules, and one draw needn't show every extreme that they name: slot_dest names every position 0 to 255 exactly once and is -1 elsewhere. Positions 2 * 8 j to 2 * 8 (j + 1) - 1 belong to the tokens of index j of seq. The slots of one index of seq name at most 2 positions of any one index of seq, and this bound is reached; one index of seq has up to 32 filled slots, reached in every draw.
All inputs are finite; a program needn't handle non-finite values.
Results may differ from a plain program's by a relative error of at most 0.0074.
Values may be sent and summed in bfloat16 or wider, within the bound.
A program may use at most 64 MiB of HBM per device.

v0:
```python
import jax
import jax.numpy as jnp
from jax import lax
from jax.sharding import PartitionSpec as P

HD = 128
SEGLEN = 64
NLEN = 64
NEIGH = 2


def shifted(shard, axis, by):
    peers = lax.axis_size(axis)
    pairs = [(i, i + by) for i in range(peers) if 0 <= i + by < peers]
    return lax.ppermute(shard, axis, pairs)


def normalize(rows, gain):
    states = rows.astype(jnp.float32)
    meansq = jnp.mean(states * states, axis=-1, keepdims=True)
    return (states * lax.rsqrt(meansq + 1e-06) * gain).astype(jnp.bfloat16)


def project(rows, weight):
    flattened = rows.reshape(-1, rows.shape[-1])
    return jnp.dot(flattened, weight, preferred_element_type=jnp.float32).astype(jnp.bfloat16)


def attend(query_win, key_win, value_win):
    windows = query_win.shape[0]
    heads = query_win.shape[2] // HD
    query_four = query_win.reshape(windows, query_win.shape[1], heads, HD)
    key_four = key_win.reshape(windows, key_win.shape[1], heads, HD)
    value_four = value_win.reshape(windows, value_win.shape[1], heads, HD)
    scores = jnp.einsum(
        "wqhd,wkhd->whqk", query_four, key_four, preferred_element_type=jnp.float32
    ) * HD ** (-0.5)
    top = jnp.max(scores, axis=-1, keepdims=True)
    exponent = jnp.exp(scores - top)
    weights = (exponent / jnp.sum(exponent, axis=-1, keepdims=True)).astype(jnp.bfloat16)
    context = jnp.einsum("whqk,wkhd->wqhd", weights, value_four, preferred_element_type=jnp.float32)
    return context.astype(jnp.bfloat16).reshape(windows, query_win.shape[1], heads * HD)


def packing(slot_dest, shards, per_shard, capacity):
    count = slot_dest.shape[0]
    is_live = slot_dest >= 0
    target = jnp.where(is_live, slot_dest // per_shard, -1)
    order = jnp.arange(count)
    earlier = (target[:, None] == target[None, :]) & (order[None, :] < order[:, None])
    slot_rank = jnp.sum(earlier.astype(jnp.int32), axis=1)
    buffer_slot = jnp.where(is_live, target * capacity + slot_rank, -1)
    matches = jnp.arange(shards * capacity)[:, None] == buffer_slot[None, :]
    selector = matches.astype(jnp.bfloat16)
    sent_dest = jnp.sum(jnp.where(matches, slot_dest[None, :] + 1, 0), axis=1) - 1
    return (selector, sent_dest.reshape(shards, capacity))


def pack(selector, rows, shards, capacity):
    flattened = rows.reshape(rows.shape[0], rows.shape[1] * rows.shape[2])
    packed = jnp.dot(selector, flattened, preferred_element_type=jnp.float32).astype(jnp.bfloat16)
    return packed.reshape(shards, capacity, rows.shape[1], rows.shape[2])


def unpack(received, received_dest, own_index, per_shard):
    flat_dest = received_dest.reshape(-1)
    local = jnp.where(flat_dest >= 0, flat_dest - own_index * per_shard, -1)
    placer = (jnp.arange(per_shard)[:, None] == local[None, :]).astype(jnp.bfloat16)
    stacked = received.reshape(flat_dest.shape[0], received.shape[2] * received.shape[3])
    placed = jnp.dot(placer, stacked, preferred_element_type=jnp.float32).astype(jnp.bfloat16)
    return placed.reshape(per_shard, received.shape[2], received.shape[3])


def edge_windows(query_rows, keys, values, prev_keys, prev_values):
    tokens_here = query_rows.shape[0]
    width = query_rows.shape[1]
    blocks = keys.shape[0]
    padded = jnp.concatenate(
        [
            jnp.zeros((1, width), jnp.bfloat16),
            query_rows,
            jnp.zeros((SEGLEN - 1, width), jnp.bfloat16),
        ],
        axis=0,
    )
    padded = padded.reshape(blocks + 1, SEGLEN, width)
    all_keys = jnp.concatenate([prev_keys[None], keys], axis=0)
    all_values = jnp.concatenate([prev_values[None], values], axis=0)
    context = attend(padded, all_keys, all_values)
    return context.reshape((blocks + 1) * SEGLEN, width)[1 : tokens_here + 1]


def on_device(queries, key_weight, value_weight, enc_gain, neighbour_states, slot_dest):
    shards = lax.axis_size("seq")
    own_index = lax.axis_index("seq")
    query_rows = queries[0]
    tokens_here = query_rows.shape[0]
    blocks = tokens_here // SEGLEN
    per_shard = NEIGH * blocks
    capacity = per_shard // shards + 1
    selector, sent_dest = packing(slot_dest, shards, per_shard, capacity)
    widened = lax.all_gather(neighbour_states, ("phase", "mp"), axis=1, tiled=True)
    received, received_dest = (
        lax.all_to_all(
            pack(selector, widened, shards, capacity),
            "seq",
            split_axis=0,
            concat_axis=0,
            tiled=True,
        ),
        lax.all_to_all(sent_dest, "seq", split_axis=0, concat_axis=0, tiled=True),
    )
    routed = unpack(received, received_dest, own_index, per_shard)
    neighbours = normalize(routed, enc_gain)
    key_mat = key_weight[0]
    value_mat = value_weight[0]
    width = key_mat.shape[1]
    keys = project(neighbours, key_mat).reshape(blocks, NEIGH * NLEN, width)
    values = project(neighbours, value_mat).reshape(blocks, NEIGH * NLEN, width)
    prev_keys, prev_values = shifted((keys[blocks - 1], values[blocks - 1]), "seq", 1)
    joined = edge_windows(query_rows, keys, values, prev_keys, prev_values)
    position = jnp.arange(tokens_here) + 1
    window_index = own_index * blocks + position // SEGLEN
    silent = (position % SEGLEN != 0) & (window_index == 0)
    result = jnp.where(silent[:, None], jnp.zeros_like(joined), joined)
    return result[None]


def solution(mesh):
    in_specs = (
        P("phase", "seq", "mp"),
        P("phase", None, "mp"),
        P("phase", None, "mp"),
        P(),
        P("seq", ("phase", "mp"), None),
        P("seq"),
    )
    out_specs = P("phase", "seq", "mp")
    return jax.shard_map(
        on_device, mesh=mesh, in_specs=in_specs, out_specs=out_specs, check_vma=False
    )
```

profile of v0, /device:TPU:8, one launch (start us, length us, event | category | flops | bytes accessed | tf_op | source)
XLA Modules:
  0.0 290.7 jit_solution(11311055246255670130)
XLA Ops:
  6.5 1.7 copy.35
  10.6 9.9 %all-to-all-start = ((s32[16,1,2]{2,1,0:T(1,128)}), s32[16,1,2]{2,1,0:T(1,128)S(1)}, u32[]{:S(2)}, u32[]{:S(2)}) async-start(s32[16,1,2]{2,1,0:T(1,128)} %bitcast), calls=%async_computation | async-start | bytes 16384 | tf_op jit(solution)/shard_map/all_to_all | solution.py:111
  20.6 52.7 %all-gather.2.cloned.1.call-done = bf16[32,64,1024]{2,0,1:T(8,128)(2,1)} async-done(((bf16[32,4,1024]{2,0,1:T(8,128)(2,1)}), bf16[32,64,1024]{2,0,1:T(8,128)(2,1)}) %all-gather.2.cloned.1.call-update) | async-done | bytes 4194320 | tf_op jit(solution)/shard_map/all_gather | solution.py:102
  73.2 2.6 copy.43
  77.1 4.3 %copy.45 = bf16[4,8,64,1024]{3,2,1,0:T(8,128)(2,1)} copy(bf16[4,8,64,1024]{3,1,2,0:T(8,128)(2,1)S(1)} %bitcast.61) | data formatting | bytes 8388608
  81.4 9.0 %all-to-all-start.1 = ((bf16[16,2,64,1024]{3,2,1,0:T(8,128)(2,1)}), bf16[16,2,64,1024]{3,2,1,0:T(8,128)(2,1)}, u32[]{:S(2)}, u32[]{:S(2)}) async-start(bf16[16,2,64,1024]{3,2,1,0:T(8,128)(2,1)} %bitcast.57), calls=%async_computation.1 | async-start | bytes 8388608 | tf_op jit(solution)/shard_map/all_to_all | solution.py:104
  90.6 93.9 %all-to-all-done.1 = bf16[16,2,64,1024]{3,2,1,0:T(8,128)(2,1)} async-done(((bf16[16,2,64,1024]{3,2,1,0:T(8,128)(2,1)}), bf16[16,2,64,1024]{3,2,1,0:T(8,128)(2,1)}, u32[]{:S(2)}, u32[]{:S(2)}) %all-to-all-start.1) | async-done | bytes 4194336 | tf_op jit(solution)/shard_map/all_to_all | solution.py:104
  184.6 4.5 %copy.46 = bf16[4,8,64,1024]{3,1,2,0:T(8,128)(2,1)S(1)} copy(bf16[4,8,64,1024]{3,2,1,0:T(8,128)(2,1)} %bitcast.16) | data formatting | bytes 8388608
  189.1 2.7 fusion.49
  191.8 4.4 %copy.47 = f32[2,8,64,1024]{3,2,1,0:T(8,128)} copy(f32[2,8,64,1024]{3,1,2,0:T(8,128)S(1)} %bitcast.59) | data formatting | bytes 8388608
  196.2 2.4 reduce_sum.38
  199.0 2.4 copy.48
  202.0 12.6 %convert_element_type.46 = bf16[1024,1024]{1,0:T(8,128)(2,1)} reshape(bf16[16,65536]{1,0:T(8,128)(2,1)S(1)} %multiply_convert_fusion) | data formatting | bytes 4194304 | tf_op jit(solution)/shard_map/convert_element_type | solution.py:21
  214.7 7.5 %fusion.18 = bf16[1024,2048]{1,0:T(8,128)(2,1)S(1)} fusion(bf16[1024,1024]{1,0:T(8,128)(2,1)} %convert_element_type.46, bf16[1,1024,2048]{2,1,0:T(8,128)(2,1)} %param.7), kind=kOutput, calls=%fused_computation.22 | convolution fusion | flops 4297064448 | bytes 10485760 | tf_op jit(solution)/shard_map/dot_general | solution.py:26
  223.0 4.3 %collective-permute-start.1 = (bf16[128,2048]{1,0:T(8,128)(2,1)}, bf16[128,2048]{1,0:T(8,128)(2,1)S(1)}, u32[]{:S(2)}, u32[]{:S(2)}) collective-permute-start(bf16[128,2048]{1,0:T(8,128)(2,1)} %slice.14), channel_id=1, source_target_pairs={{0,2},{2,4},{4,6},{6,8},{8,10},{10,12},{12,14},{14,16},{16,18},{18... | collective-permute-start | bytes 1572872 | tf_op jit(solution)/shard_map/ppermute | solution.py:15
  227.3 4.7 %fusion.15 = bf16[1024,2048]{1,0:T(8,128)(2,1)S(1)} fusion(bf16[1024,1024]{1,0:T(8,128)(2,1)S(1)} %copy-done.9, bf16[1,1024,2048]{2,1,0:T(8,128)(2,1)S(1)} %copy-done.10), kind=kOutput, calls=%fused_computation.21 | convolution fusion | flops 4297064448 | bytes 10485760 | tf_op jit(solution)/shard_map/dot_general | solution.py:26
  234.2 2.6 collective-permute-start
  240.6 3.2 %copy.38 = bf16[8,128,16,128]{3,1,2,0:T(8,128)(2,1)} copy(bf16[8,128,16,128]{3,2,1,0:T(8,128)(2,1)S(1)} %bitcast.64) | data formatting | bytes 8388608 | tf_op jit(solution)/shard_map/concatenate | solution.py:88
  246.7 5.0 %collective-permute-done = bf16[128,2048]{1,0:T(8,128)(2,1)S(1)} collective-permute-done((bf16[128,2048]{1,0:T(8,128)(2,1)}, bf16[128,2048]{1,0:T(8,128)(2,1)S(1)}, u32[]{:S(2)}, u32[]{:S(2)}) %collective-permute-start) | collective-permute-done | bytes 524320 | tf_op jit(solution)/shard_map/ppermute | solution.py:15
  252.0 3.3 %fusion.2 = f32[9,16,64,128]{3,2,1,0:T(8,128)S(1)} fusion(bf16[8,128,16,128]{3,1,2,0:T(8,128)(2,1)S(1)} %copy.40, bf16[1,128,16,128]{3,1,2,0:T(8,128)(2,1)S(1)} %copy.39, bf16[9,64,16,128]{3,2,1,0:T(8,128)(2,1)S(1)} %bitcast.68), kind=kOutput, calls=%fused_computation.4 | convolution fusion | flops 304349184 | bytes 11796480 | tf_op jit(solution)/shard_map/wqhd,wkhd->whqk/dot_general | solution.py:35
  255.3 2.1 copy-done.7
  257.4 2.5 fusion.50
  259.9 19.4 %convert_bitcast_fusion = bf16[9,64,16,128]{3,1,2,0:T(8,128)(2,1)S(1)} fusion(bf16[8,128,16,128]{3,1,2,0:T(8,128)(2,1)} %copy.38, bf16[1,128,16,128]{3,1,2,0:T(8,128)(2,1)S(1)} %copy.37, f32[9,16,64]{2,1,0:T(8,128)S(1)} %fusion.50, f32[9,16,64,128]{3,2,1,0:T(8,128)} %copy-done.7), kind=kOutput, calls=%fused_computation.26 | convolution fusion | flops 318514304 | bytes 11833344 | tf_op jit(solution)/shard_map/whqk,wkhd->wqhd/dot_general | solution.py:41
  281.6 2.0 fusion.26
  (56 shorter events, 16.8 us)
Async XLA Ops:
  6.5 83.9 %copy-start = (f32[1024]{0:T(1024)S(1)}, f32[1024]{0:T(1024)}, u32[]{:S(2)}) copy-start(f32[1024]{0:T(1024)} %param.9) | copy-start | bytes 12292
  6.5 66.7 %all-gather.2.cloned.1.call-start = ((), (), s32[]{:S(2)}) async-start(), calls=%async_computation.2 | async-start | bytes 4456448 | tf_op jit(solution)/shard_map/all_gather | solution.py:102
  10.6 70.7 %all-to-all-start = ((s32[16,1,2]{2,1,0:T(1,128)}), s32[16,1,2]{2,1,0:T(1,128)S(1)}, u32[]{:S(2)}, u32[]{:S(2)}) async-start(s32[16,1,2]{2,1,0:T(1,128)} %bitcast), calls=%async_computation | async-start | bytes 16384 | tf_op jit(solution)/shard_map/all_to_all | solution.py:111
  81.4 103.2 %all-to-all-start.1 = ((bf16[16,2,64,1024]{3,2,1,0:T(8,128)(2,1)}), bf16[16,2,64,1024]{3,2,1,0:T(8,128)(2,1)}, u32[]{:S(2)}, u32[]{:S(2)}) async-start(bf16[16,2,64,1024]{3,2,1,0:T(8,128)(2,1)} %bitcast.57), calls=%async_computation.1 | async-start | bytes 8388608 | tf_op jit(solution)/shard_map/all_to_all | solution.py:104
  199.0 2.4 copy-start.2
  214.6 12.7 %copy-start.9 = (bf16[1024,1024]{1,0:T(8,128)(2,1)S(1)}, bf16[1024,1024]{1,0:T(8,128)(2,1)}, u32[]{:S(2)}) copy-start(bf16[1024,1024]{1,0:T(8,128)(2,1)} %convert_element_type.46) | copy-start | bytes 6291460
  214.6 12.7 %copy-start.10 = (bf16[1,1024,2048]{2,1,0:T(8,128)(2,1)S(1)}, bf16[1,1024,2048]{2,1,0:T(8,128)(2,1)}, u32[]{:S(2)}) copy-start(bf16[1,1024,2048]{2,1,0:T(8,128)(2,1)} %param.8) | copy-start | bytes 12582916
  222.1 9.9 %copy-start.3 = (bf16[1024,2048]{1,0:T(8,128)(2,1)}, bf16[1024,2048]{1,0:T(8,128)(2,1)S(1)}, u32[]{:S(2)}) copy-start(bf16[1024,2048]{1,0:T(8,128)(2,1)S(1)} %fusion.18) | copy-start | bytes 12582916
  223.0 14.0 %copy-start.8 = (bf16[1,512,2048]{2,1,0:T(8,128)(2,1)S(1)}, bf16[1,512,2048]{2,1,0:T(8,128)(2,1)}, u32[]{:S(2)}) copy-start(bf16[1,512,2048]{2,1,0:T(8,128)(2,1)} %param.6) | copy-start | bytes 6291460
  223.0 23.4 %collective-permute-start.1 = (bf16[128,2048]{1,0:T(8,128)(2,1)}, bf16[128,2048]{1,0:T(8,128)(2,1)S(1)}, u32[]{:S(2)}, u32[]{:S(2)}) collective-permute-start(bf16[128,2048]{1,0:T(8,128)(2,1)} %slice.14), channel_id=1, source_target_pairs={{0,2},{2,4},{4,6},{6,8},{8,10},{10,12},{12,14},{14,16},{16,18},{18... | collective-permute-start | bytes 1572872 | tf_op jit(solution)/shard_map/ppermute | solution.py:15
  232.0 2.2 copy-start.5
  234.2 17.5 %collective-permute-start = (bf16[128,2048]{1,0:T(8,128)(2,1)}, bf16[128,2048]{1,0:T(8,128)(2,1)S(1)}, u32[]{:S(2)}, u32[]{:S(2)}) collective-permute-start(bf16[128,2048]{1,0:T(8,128)(2,1)} %slice.15), channel_id=1, source_target_pairs={{0,2},{2,4},{4,6},{6,8},{8,10},{10,12},{12,14},{14,16},{16,18},{18... | collective-permute-start | bytes 1572872 | tf_op jit(solution)/shard_map/ppermute | solution.py:15
  237.0 2.2 copy-start.6
  240.6 3.2 %copy-start.4 = (bf16[1024,2048]{1,0:T(8,128)(2,1)S(1)}, bf16[1024,2048]{1,0:T(8,128)(2,1)}, u32[]{:S(2)}) copy-start(bf16[1024,2048]{1,0:T(8,128)(2,1)} %copy-done.3) | copy-start | bytes 12582916
  255.3 2.1 copy-start.7
  281.0 2.6 copy-start.1
Sparse Core Ops, SparseCore 0:
  10.1 63.1 all-gather.1
where the time goes:
time: 295 us; the launch traced here: 291 us
  waiting for transfers between devices  152 us (52%)
  local copies, waits for them, and re-layouts  50.1 us (17%)
  matrix products  38.8 us (13%)
  starting transfers between devices  25.9 us (9%)
  between operations  14 us (5%)
  other arithmetic  10.3 us (3%)
    all_to_all x1, waiting for transfers between devices, on_device(): lax.all_to_all(pack(selector, widened, shards, capacity), 'seq', split_ax...  93.9 us
    all_gather x1, waiting for transfers between devices, on_device(): lax.all_gather(neighbour_states, ('phase', 'mp'), axis=1, tiled=True)  52.7 us
    unnamed x35, local copies, waits for them, and re-layouts  25.6 us
    dot_general x1, matrix products, attend(): jnp.einsum('whqk,wkhd->wqhd', weights, value_four, preferred_element_type...  19.4 us
    convert_element_type x1, local copies, waits for them, and re-layouts, normalize(): return (states * lax.rsqrt(meansq + 1e-06) * gain).astype(jnp.bfloat16)  12.6 us
    dot_general x2, matrix products, project(): jnp.dot(flattened, weight, preferred_element_type=jnp.float32)  12.2 us
    all_to_all x1, starting transfers between devices, on_device(): lax.all_to_all(sent_dest, 'seq', split_axis=0, concat_axis=0, tiled=True)  9.94 us
    all_to_all x1, starting transfers between devices, on_device(): lax.all_to_all(pack(selector, widened, shards, capacity), 'seq', split_ax...  9.02 us
  transfers between devices with their start and end apart: 5, of which 3 were waited for; matrix products, arithmetic and copies ran while one was open for 9% of the time, Pallas kernels for 0%

commit v1 on v0

v1 whole, which is shorter than its diff:
```python
import jax
import jax.numpy as jnp
from jax import lax
from jax.experimental import pallas as pl
from jax.experimental.pallas import tpu as pltpu
from jax.sharding import PartitionSpec as P

MESH = pl.DeviceIdType.MESH
BF = jnp.bfloat16
F32 = jnp.float32

HD = 128
SEGLEN = 64
SEQ = 16
CHIPS = 8
CHUNKS = 4
ORDER = (1, 0, 2, 3)
EXP2_SCALE = HD ** (-0.5) * 1.4426950408889634


def iota(shape, dim):
    return lax.broadcasted_iota(jnp.int32, shape, dim)


def pack_rows(states_ref, gain_ref, dest_ref, sbuf):
    states = states_ref[...].astype(F32)
    meansq = jnp.mean(states * states, axis=-1, keepdims=True)
    normed = states * lax.rsqrt(meansq + 1e-06) * gain_ref[...].reshape(1, 1, -1)
    dest = dest_ref[...]
    row = iota((128, 32), 0)
    hit = lax.shift_right_arithmetic(dest, 4) == row // 8
    before = (iota((32, 32), 0) < iota((32, 32), 1)).astype(BF)
    rank = jnp.dot(hit.astype(BF), before, preferred_element_type=F32)
    pick = hit & (rank == ((row // 4) % 2).astype(F32))
    place = jnp.sum(jnp.where(pick, (dest + 1).astype(F32), 0.0), axis=1, keepdims=True)
    packed = jnp.zeros((128, 1024), F32)
    for r in range(4):
        one = (pick & (row % 4 == r)).astype(BF)
        packed += jnp.dot(one, normed[:, r, :].astype(BF), preferred_element_type=F32)
    left = packed[:, :512].reshape(SEQ, 8, 512)
    right = packed[:, 512:].reshape(SEQ, 8, 512)
    place = jnp.broadcast_to(place, (128, 128)).reshape(SEQ, 8, 128)
    sbuf[:, :, 0:512] = jnp.concatenate([left, right], axis=1).astype(BF)
    sbuf[:, :, 512:640] = jnp.concatenate([place, place], axis=1).astype(BF)


def unpack_rows(rbuf, me, piece):
    got = rbuf[...].astype(F32)
    place = got[:, :8, 512:].reshape(128, 128)
    row, lane = iota((128, 128), 0), iota((128, 128), 1)
    want = SEQ * me + 2 * (lane // 8 - 1) + (lane // 4) % 2 + 1
    match = (place == want.astype(F32)) & (row % 4 == lane % 4) & (lane >= 8) & (lane < 72)
    match = match.astype(BF)
    for half in range(2):
        rows = got[:, 8 * half : 8 * half + 8, :512].reshape(128, 512).astype(BF)
        out = lax.dot_general(match, rows, (((0,), (0,)), ((), ())), preferred_element_type=F32)
        piece[:, 512 * half : 512 * half + 512] = out[:80].astype(BF)


def by_window(rows):
    four = rows.reshape(16, 2, 8, rows.shape[1])
    return [four[:, w].reshape(128, rows.shape[1]).astype(BF) for w in range(2)]


def attend(c, n, me, gath, wk, wv, qs, outs):
    cols = pl.ds(pl.multiple_of(n * 256, 256), 256)
    near = gath[c].reshape(256, 1024)
    key = jnp.concatenate(by_window(jnp.dot(near, wk[:, cols], preferred_element_type=F32)), axis=0)
    val = jnp.concatenate(by_window(jnp.dot(near, wv[:, cols], preferred_element_type=F32)), axis=0)
    last = iota((16, 256), 0) == 15
    zero = jnp.zeros((SEGLEN, HD), BF)
    left = []
    for w in range(2):
        at = SEGLEN * (2 * c + w)
        head = qs[at + 16 : at + 64, cols]
        tail = jnp.where(last, qs[at : at + 16, cols], qs[at + 64 : at + 80, cols])
        query = jnp.concatenate([head, tail], axis=0)
        left.append(jnp.concatenate([query[:, :HD], zero], axis=1))
        left.append(jnp.concatenate([zero, query[:, HD:]], axis=1))
    scores = lax.dot_general(
        jnp.concatenate(left, axis=0), key, (((1,), (1,)), ((), ())), preferred_element_type=F32
    )
    weights = []
    for w in range(2):
        own = scores[128 * w : 128 * w + 128, 128 * w : 128 * w + 128]
        top = jnp.max(own, axis=-1, keepdims=True)
        exponent = jnp.exp2((own - top) * EXP2_SCALE)
        total = jnp.sum(exponent, axis=-1, keepdims=True)
        own = (exponent * (1.0 / total)).astype(BF)
        pad = jnp.zeros((128, 128), BF)
        weights.append(jnp.concatenate([own, pad] if w == 0 else [pad, own], axis=1))
    context = jnp.dot(jnp.concatenate(weights, axis=0), val, preferred_element_type=F32)
    for w in range(2):
        at = SEGLEN * (2 * c + w)
        two = context[128 * w : 128 * w + 128]
        both = jnp.concatenate([two[:SEGLEN, :HD], two[SEGLEN:, HD:]], axis=1)
        if c == 0 and w == 0:
            keep = (iota((SEGLEN, 256), 0) == SEGLEN - 1) | (me > 0)
            both = jnp.where(keep, both, 0.0)
        both = both.astype(BF)
        outs[at + 16 : at + 64, cols] = both[:48]
        outs[at : at + 16, cols] = jnp.where(last, both[48:], outs[at : at + 16, cols])
        outs[at + 64 : at + 80, cols] = jnp.where(last, outs[at + 64 : at + 80, cols], both[48:])


def kernel(
    q_hbm, wk_hbm, wv_hbm, gain_ref, states_ref, dest_ref, out_hbm,
    sbuf, rbuf, piece, prev, gath, wk, wv, qs, outs, back,
    load_sem, route_send, route_recv, halo_send, halo_recv, gath_send, gath_recv, pair_send, pair_recv,
):
    phase, me, mp = lax.axis_index("phase"), lax.axis_index("seq"), lax.axis_index("mp")
    x, core = phase // 2, phase % 2
    chip = x * 2 + mp

    def at_seq(s):
        return (phase, s, mp)

    def at_chip(k):
        return ((k // 2) * 2 + core, me, k % 2)

    after, ahead = lax.rem(me + 1, SEQ), lax.rem(me + SEQ - 1, SEQ)
    partner = (x * 2 + 1 - core, me, mp)
    barrier = pltpu.get_barrier_semaphore()
    for off in range(1, SEQ):
        pl.semaphore_signal(barrier, inc=1, device_id=at_seq(lax.rem(me + off, SEQ)), device_id_type=MESH)
    for off in range(1, CHIPS):
        pl.semaphore_signal(barrier, inc=1, device_id=at_chip(lax.rem(chip + off, CHIPS)), device_id_type=MESH)
    pl.semaphore_signal(barrier, inc=1, device_id=partner, device_id_type=MESH)

    loads = [
        pltpu.make_async_copy(q_hbm.at[0], qs.at[pl.ds(16, 512)], load_sem.at[0]),
        pltpu.make_async_copy(wk_hbm.at[0], wk, load_sem.at[1]),
        pltpu.make_async_copy(wv_hbm.at[0], wv, load_sem.at[2]),
    ]
    for load in loads:
        load.start()
    pack_rows(states_ref, gain_ref, dest_ref, sbuf)
    outs[0:16] = jnp.zeros((16, 2048), BF)
    pl.semaphore_wait(barrier, SEQ - 1 + CHIPS - 1 + 1)

    def route(s, slot):
        return pltpu.make_async_remote_copy(
            src_ref=sbuf.at[s], dst_ref=rbuf.at[slot], send_sem=route_send.at[s], recv_sem=route_recv.at[slot],
            device_id=at_seq(s), device_id_type=MESH,
        )

    for off in range(1, SEQ):
        route(lax.rem(me + off, SEQ), me).start()
    query_halo = pltpu.make_async_remote_copy(
        src_ref=q_hbm.at[0, pl.ds(496, 16)], dst_ref=qs.at[pl.ds(0, 16)],
        send_sem=halo_send.at[0], recv_sem=halo_recv.at[0], device_id=at_seq(after), device_id_type=MESH,
    )
    query_halo.start()
    rbuf[me] = sbuf[me]
    for off in range(1, SEQ):
        s = lax.rem(me + SEQ - off, SEQ)
        route(s, s).wait_recv()
    unpack_rows(rbuf, me, piece)

    prev_halo = pltpu.make_async_remote_copy(
        src_ref=piece.at[pl.ds(64, 16)], dst_ref=prev,
        send_sem=halo_send.at[1], recv_sem=halo_recv.at[1], device_id=at_seq(after), device_id_type=MESH,
    )
    prev_halo.start()

    def give(c, k, slot):
        return pltpu.make_async_remote_copy(
            src_ref=gath.at[c, core, chip], dst_ref=gath.at[c, core, slot],
            send_sem=gath_send.at[c, k], recv_sem=gath_recv.at[c, slot],
            device_id=at_chip(k), device_id_type=MESH,
        )

    def across(c, side):
        return pltpu.make_async_remote_copy(
            src_ref=gath.at[c, core], dst_ref=gath.at[c, side], send_sem=pair_send.at[c], recv_sem=pair_recv.at[c],
            device_id=partner, device_id_type=MESH,
        )

    for c in ORDER:
        if c == 0:
            prev_halo.wait_recv()
            mine = jnp.where(iota((16, 1024), 0) < 8, prev[...], piece[0:16])
        else:
            mine = piece[16 * c : 16 * c + 16]
        gath[c, core, chip] = mine
        for off in range(1, CHIPS):
            give(c, lax.rem(chip + off, CHIPS), chip).start()

    def pass_on(c):
        for off in range(1, CHIPS):
            k = lax.rem(chip + CHIPS - off, CHIPS)
            give(c, k, k).wait_recv()
        across(c, core).start()

    ctx_halo = pltpu.make_async_remote_copy(
        src_ref=outs.at[pl.ds(0, 16)], dst_ref=back,
        send_sem=halo_send.at[2], recv_sem=halo_recv.at[2], device_id=at_seq(ahead), device_id_type=MESH,
    )
    pass_on(ORDER[0])
    for load in loads:
        load.wait()
    query_halo.wait_recv()
    for i, c in enumerate(ORDER):
        across(c, 1 - core).wait_recv()

        def step(n, carry, c=c):
            attend(c, n, me, gath, wk, wv, qs, outs)
            return carry

        lax.fori_loop(0, 4, step, 0)
        if i + 1 < CHUNKS:
            pass_on(ORDER[i + 1])
        lax.fori_loop(4, 8, step, 0)
        if c == 0:
            ctx_halo.start()

    ctx_halo.wait_recv()
    outs[512:528] = jnp.where(iota((16, 2048), 0) == 15, back[...], outs[512:528])
    store = pltpu.make_async_copy(outs.at[pl.ds(16, 512)], out_hbm.at[0], load_sem.at[3])
    store.start()
    for off in range(1, SEQ):
        route(lax.rem(me + off, SEQ), me).wait_send()
    query_halo.wait_send()
    prev_halo.wait_send()
    ctx_halo.wait_send()
    for c in ORDER:
        for off in range(1, CHIPS):
            give(c, lax.rem(chip + off, CHIPS), chip).wait_send()
        across(c, core).wait_send()
    store.wait()


def on_device(queries, key_weight, value_weight, enc_gain, neighbour_states, slot_dest):
    whole = pl.BlockSpec(memory_space=pltpu.VMEM)
    place = pl.BlockSpec(memory_space=pl.ANY)
    dma = pltpu.SemaphoreType.DMA
    return pl.pallas_call(
        kernel,
        out_shape=jax.ShapeDtypeStruct(queries.shape, BF),
        in_specs=[place, place, place, whole, whole, whole],
        out_specs=place,
        scratch_shapes=[
            pltpu.VMEM((SEQ, 16, 640), BF),
            pltpu.VMEM((SEQ, 16, 640), BF),
            pltpu.VMEM((80, 1024), BF),
            pltpu.VMEM((16, 1024), BF),
            pltpu.VMEM((CHUNKS, 2, CHIPS, 16, 1024), BF),
            pltpu.VMEM((1024, 2048), BF),
            pltpu.VMEM((1024, 2048), BF),
            pltpu.VMEM((528, 2048), BF),
            pltpu.VMEM((528, 2048), BF),
            pltpu.VMEM((16, 2048), BF),
            dma((4,)),
            dma((SEQ,)),
            dma((SEQ,)),
            dma((3,)),
            dma((3,)),
            dma((CHUNKS, CHIPS)),
            dma((CHUNKS, CHIPS)),
            dma((CHUNKS,)),
            dma((CHUNKS,)),
        ],
        compiler_params=pltpu.CompilerParams(
            collective_id=0, has_side_effects=True, vmem_limit_bytes=44 * 1024 * 1024
        ),
    )(
        queries, key_weight, value_weight, enc_gain.reshape(1, -1), neighbour_states, slot_dest.reshape(1, -1),
    )


def solution(mesh):
    in_specs = (
        P("phase", "seq", "mp"),
        P("phase", None, "mp"),
        P("phase", None, "mp"),
        P(),
        P("seq", ("phase", "mp"), None),
        P("seq"),
    )
    out_specs = P("phase", "seq", "mp")
    return jax.shard_map(
        on_device, mesh=mesh, in_specs=in_specs, out_specs=out_specs, check_vma=False
    )
```

time: 295 us -> 69.4 us (0.24)
  the two profiles are of different devices: /device:TPU:8 before, /device:TPU:1 now
where the time goes in v1:
time: 69.4 us; the launch traced here: 68.2 us
  Pallas kernels  60.8 us (88%)
  local copies, waits for them, and re-layouts  7.39 us (11%)
    pallas_call x1, Pallas kernels, on_device(): pl.pallas_call(kernel, out_shape=jax.ShapeDtypeStruct(queries.shape, BF),...  60.8 us
    unnamed x11, local copies, waits for them, and re-layouts  7.39 us

profile of v1, /device:TPU:1, one launch (start us, length us, event | category | flops | bytes accessed | tf_op | source)
XLA Modules:
  0.0 68.2 jit_solution(1772124251239501872)
XLA Ops:
  0.0 0.0 copy-start
  0.0 2.2 %copy-done = bf16[1,1024,2048]{2,1,0:T(8,128)(2,1)S(1)} copy-done((bf16[1,1024,2048]{2,1,0:T(8,128)(2,1)S(1)}, bf16[1,1024,2048]{2,1,0:T(8,128)(2,1)}, u32[]{:S(2)}) %copy-start) | copy-done | bytes 4194328
  2.2 0.0 copy-start.1
  2.2 1.6 %copy-done.1 = bf16[1,512,2048]{2,1,0:T(8,128)(2,1)S(1)} copy-done((bf16[1,512,2048]{2,1,0:T(8,128)(2,1)S(1)}, bf16[1,512,2048]{2,1,0:T(8,128)(2,1)}, u32[]{:S(2)}) %copy-start.1) | copy-done | bytes 2097176
  3.8 0.0 copy-start.2
  3.8 0.9 %copy-done.2 = bf16[32,4,1024]{2,1,0:T(4,128)(2,1)S(1)} copy-done((bf16[32,4,1024]{2,1,0:T(4,128)(2,1)S(1)}, bf16[32,4,1024]{2,1,0:T(4,128)(2,1)}, u32[]{:S(2)}) %copy-start.2) | copy-done | bytes 262168
  4.7 0.0 copy-start.3
  4.7 0.7 %copy-done.3 = f32[1024]{0:T(1024)S(1)} copy-done((f32[1024]{0:T(1024)S(1)}, f32[1024]{0:T(1024)}, u32[]{:S(2)}) %copy-start.3) | copy-done | bytes 4120
  5.4 0.0 copy-start.4
  5.4 0.7 copy-done.4
  6.1 60.8 %shard_map.64 = bf16[1,512,2048]{2,1,0:T(8,128)(2,1)S(1)} custom-call(bf16[1,512,2048]{2,1,0:T(8,128)(2,1)S(1)} %copy-done.1, bf16[1,1024,2048]{2,1,0:T(8,128)(2,1)S(1)} %copy-done, bf16[1,1024,2048]{2,1,0:T(8,128)(2,1)} %wv_hbm.1, f32[1,1024]{1,0:T(1,128)S(1)} %bitcast.2, bf16[32,4,1024]{2,1,0:T(4,128)(2,1)S(1)} %copy-done.2, s32[1,32]{1,0:T(1,128)S(1)} %bitcast.3), custom_call_target="tpu_custom_call" | custom-call | tf_op jit(solution)/shard_map/pallas_call | solution.py:237
  66.9 1.3 %copy.8 = bf16[1,512,2048]{2,1,0:T(8,128)(2,1)} copy(bf16[1,512,2048]{2,1,0:T(8,128)(2,1)S(1)} %shard_map.64) | data formatting | bytes 4194304
Async XLA Ops:
  0.0 2.2 %copy-start = (bf16[1,1024,2048]{2,1,0:T(8,128)(2,1)S(1)}, bf16[1,1024,2048]{2,1,0:T(8,128)(2,1)}, u32[]{:S(2)}) copy-start(bf16[1,1024,2048]{2,1,0:T(8,128)(2,1)} %wk_hbm.1) | copy-start | bytes 12582916
  2.2 1.6 %copy-start.1 = (bf16[1,512,2048]{2,1,0:T(8,128)(2,1)S(1)}, bf16[1,512,2048]{2,1,0:T(8,128)(2,1)}, u32[]{:S(2)}) copy-start(bf16[1,512,2048]{2,1,0:T(8,128)(2,1)} %q_hbm.1) | copy-start | bytes 6291460
  3.8 0.9 %copy-start.2 = (bf16[32,4,1024]{2,1,0:T(4,128)(2,1)S(1)}, bf16[32,4,1024]{2,1,0:T(4,128)(2,1)}, u32[]{:S(2)}) copy-start(bf16[32,4,1024]{2,1,0:T(4,128)(2,1)} %states_ref.1) | copy-start | bytes 786436
  4.7 0.7 %copy-start.3 = (f32[1024]{0:T(1024)S(1)}, f32[1024]{0:T(1024)}, u32[]{:S(2)}) copy-start(f32[1024]{0:T(1024)} %param.9) | copy-start | bytes 12292
  5.4 0.7 copy-start.4

commit v2 on v1

--- a/solution.py
+++ b/solution.py
@@ -22,7 +22,7 @@
     return lax.broadcasted_iota(jnp.int32, shape, dim)
 
 
-def pack_rows(states_ref, gain_ref, dest_ref, sbuf):
+def pack_rows(states_ref, gain_ref, dest_ref, sbuf, mbuf):
     states = states_ref[...].astype(F32)
     meansq = jnp.mean(states * states, axis=-1, keepdims=True)
     normed = states * lax.rsqrt(meansq + 1e-06) * gain_ref[...].reshape(1, 1, -1)
@@ -32,27 +32,35 @@
     before = (iota((32, 32), 0) < iota((32, 32), 1)).astype(BF)
     rank = jnp.dot(hit.astype(BF), before, preferred_element_type=F32)
     pick = hit & (rank == ((row // 4) % 2).astype(F32))
-    place = jnp.sum(jnp.where(pick, (dest + 1).astype(F32), 0.0), axis=1, keepdims=True)
     packed = jnp.zeros((128, 1024), F32)
     for r in range(4):
         one = (pick & (row % 4 == r)).astype(BF)
         packed += jnp.dot(one, normed[:, r, :].astype(BF), preferred_element_type=F32)
     left = packed[:, :512].reshape(SEQ, 8, 512)
     right = packed[:, 512:].reshape(SEQ, 8, 512)
-    place = jnp.broadcast_to(place, (128, 128)).reshape(SEQ, 8, 128)
-    sbuf[:, :, 0:512] = jnp.concatenate([left, right], axis=1).astype(BF)
-    sbuf[:, :, 512:640] = jnp.concatenate([place, place], axis=1).astype(BF)
-
-
-def unpack_rows(rbuf, me, piece):
+    sbuf[...] = jnp.concatenate([left, right], axis=1).astype(BF)
+    hit = lax.shift_right_arithmetic(dest, 4) == iota((SEQ, 32), 0)
+    rank = jnp.dot(hit.astype(BF), before, preferred_element_type=F32)
+    first, second = [
+        jnp.sum(jnp.where(hit & (rank == k), dest + 1, 0), axis=1, keepdims=True) for k in (0.0, 1.0)
+    ]
+    lane = iota((SEQ, 128), 1)
+    place = jnp.where(lane == 0, first, jnp.where(lane == 1, second, 0))
+    for d in range(SEQ):
+        mbuf[d] = place[d : d + 1]
+
+
+def unpack_rows(rbuf, mrec, me, piece):
+    row, lane = iota((128, 128), 0), iota((128, 128), 1)
+    source = (iota((128, SEQ), 0) // 8 == iota((128, SEQ), 1)).astype(BF)
+    place = jnp.dot(source, mrec[:, 0, :].astype(F32).astype(BF), preferred_element_type=F32)
+    place = jnp.sum(jnp.where(lane == (row // 4) % 2, place, 0.0), axis=1, keepdims=True)
     got = rbuf[...].astype(F32)
-    place = got[:, :8, 512:].reshape(128, 128)
-    row, lane = iota((128, 128), 0), iota((128, 128), 1)
     want = SEQ * me + 2 * (lane // 8 - 1) + (lane // 4) % 2 + 1
     match = (place == want.astype(F32)) & (row % 4 == lane % 4) & (lane >= 8) & (lane < 72)
     match = match.astype(BF)
     for half in range(2):
-        rows = got[:, 8 * half : 8 * half + 8, :512].reshape(128, 512).astype(BF)
+        rows = got[:, 8 * half : 8 * half + 8].reshape(128, 512).astype(BF)
         out = lax.dot_general(match, rows, (((0,), (0,)), ((), ())), preferred_element_type=F32)
         piece[:, 512 * half : 512 * half + 512] = out[:80].astype(BF)
 
@@ -62,51 +70,59 @@
     return [four[:, w].reshape(128, rows.shape[1]).astype(BF) for w in range(2)]
 
 
-def attend(c, n, me, gath, wk, wv, qs, outs):
-    cols = pl.ds(pl.multiple_of(n * 256, 256), 256)
+def attend(c, gath, wk, wv, qs, outs):
     near = gath[c].reshape(256, 1024)
-    key = jnp.concatenate(by_window(jnp.dot(near, wk[:, cols], preferred_element_type=F32)), axis=0)
-    val = jnp.concatenate(by_window(jnp.dot(near, wv[:, cols], preferred_element_type=F32)), axis=0)
     last = iota((16, 256), 0) == 15
     zero = jnp.zeros((SEGLEN, HD), BF)
-    left = []
-    for w in range(2):
-        at = SEGLEN * (2 * c + w)
-        head = qs[at + 16 : at + 64, cols]
-        tail = jnp.where(last, qs[at : at + 16, cols], qs[at + 64 : at + 80, cols])
-        query = jnp.concatenate([head, tail], axis=0)
-        left.append(jnp.concatenate([query[:, :HD], zero], axis=1))
-        left.append(jnp.concatenate([zero, query[:, HD:]], axis=1))
-    scores = lax.dot_general(
-        jnp.concatenate(left, axis=0), key, (((1,), (1,)), ((), ())), preferred_element_type=F32
-    )
-    weights = []
-    for w in range(2):
-        own = scores[128 * w : 128 * w + 128, 128 * w : 128 * w + 128]
-        top = jnp.max(own, axis=-1, keepdims=True)
-        exponent = jnp.exp2((own - top) * EXP2_SCALE)
-        total = jnp.sum(exponent, axis=-1, keepdims=True)
-        own = (exponent * (1.0 / total)).astype(BF)
-        pad = jnp.zeros((128, 128), BF)
-        weights.append(jnp.concatenate([own, pad] if w == 0 else [pad, own], axis=1))
-    context = jnp.dot(jnp.concatenate(weights, axis=0), val, preferred_element_type=F32)
-    for w in range(2):
-        at = SEGLEN * (2 * c + w)
-        two = context[128 * w : 128 * w + 128]
-        both = jnp.concatenate([two[:SEGLEN, :HD], two[SEGLEN:, HD:]], axis=1)
-        if c == 0 and w == 0:
-            keep = (iota((SEGLEN, 256), 0) == SEGLEN - 1) | (me > 0)
-            both = jnp.where(keep, both, 0.0)
-        both = both.astype(BF)
-        outs[at + 16 : at + 64, cols] = both[:48]
-        outs[at : at + 16, cols] = jnp.where(last, both[48:], outs[at : at + 16, cols])
-        outs[at + 64 : at + 80, cols] = jnp.where(last, outs[at + 64 : at + 80, cols], both[48:])
+    pad = jnp.zeros((128, 128), BF)
+    pairs = range(8)
+    at = [pl.multiple_of(SEGLEN * (2 * c + w), SEGLEN) for w in range(2)]
+    cols = [pl.ds(256 * n, 256) for n in pairs]
+
+    def project(weight, n):
+        return jnp.concatenate(by_window(jnp.dot(near, weight[:, cols[n]], preferred_element_type=F32)), axis=0)
+
+    def score(n, key):
+        left = []
+        for w in range(2):
+            head = qs[pl.ds(at[w] + 16, 48), cols[n]]
+            tail = jnp.where(last, qs[pl.ds(at[w], 16), cols[n]], qs[pl.ds(at[w] + 64, 16), cols[n]])
+            query = jnp.concatenate([head, tail], axis=0)
+            left.append(jnp.concatenate([query[:, :HD], zero], axis=1))
+            left.append(jnp.concatenate([zero, query[:, HD:]], axis=1))
+        return lax.dot_general(
+            jnp.concatenate(left, axis=0), key, (((1,), (1,)), ((), ())), preferred_element_type=F32
+        )
+
+    def finish(n, scores, val):
+        weights = []
+        for w in range(2):
+            own = scores[128 * w : 128 * w + 128, 128 * w : 128 * w + 128]
+            top = jnp.max(own, axis=-1, keepdims=True)
+            exponent = jnp.exp2((own - top) * EXP2_SCALE)
+            total = jnp.sum(exponent, axis=-1, keepdims=True)
+            own = (exponent * (1.0 / total)).astype(BF)
+            weights.append(jnp.concatenate([own, pad] if w == 0 else [pad, own], axis=1))
+        context = jnp.dot(jnp.concatenate(weights, axis=0), val, preferred_element_type=F32)
+        for w in range(2):
+            two = context[128 * w : 128 * w + 128]
+            both = jnp.concatenate([two[:SEGLEN, :HD], two[SEGLEN:, HD:]], axis=1)
+            both = both.astype(BF)
+            outs[pl.ds(at[w] + 16, 48), cols[n]] = both[:48]
+            outs[pl.ds(at[w], 16), cols[n]] = jnp.where(last, both[48:], outs[pl.ds(at[w], 16), cols[n]])
+            outs[pl.ds(at[w] + 64, 16), cols[n]] = jnp.where(last, outs[pl.ds(at[w] + 64, 16), cols[n]], both[48:])
+
+    keys = [project(wk, n) for n in pairs]
+    scores = [score(n, keys[n]) for n in pairs]
+    vals = [project(wv, n) for n in pairs]
+    for n in pairs:
+        finish(n, scores[n], vals[n])
 
 
 def kernel(
     q_hbm, wk_hbm, wv_hbm, gain_ref, states_ref, dest_ref, out_hbm,
-    sbuf, rbuf, piece, prev, gath, wk, wv, qs, outs, back,
-    load_sem, route_send, route_recv, halo_send, halo_recv, gath_send, gath_recv, pair_send, pair_recv,
+    sbuf, rbuf, mbuf, mrec, piece, prev, gath, wk, wv, qs, outs, back,
+    load_sem, route_send, route_recv, meta_send, meta_recv, halo_send, halo_recv, gath_send, gath_recv, pair_send, pair_recv,
 ):
     phase, me, mp = lax.axis_index("phase"), lax.axis_index("seq"), lax.axis_index("mp")
     x, core = phase // 2, phase % 2
@@ -134,7 +150,7 @@
     ]
     for load in loads:
         load.start()
-    pack_rows(states_ref, gain_ref, dest_ref, sbuf)
+    pack_rows(states_ref, gain_ref, dest_ref, sbuf, mbuf)
     outs[0:16] = jnp.zeros((16, 2048), BF)
     pl.semaphore_wait(barrier, SEQ - 1 + CHIPS - 1 + 1)
 
@@ -144,7 +160,14 @@
             device_id=at_seq(s), device_id_type=MESH,
         )
 
+    def inform(s, slot):
+        return pltpu.make_async_remote_copy(
+            src_ref=mbuf.at[s], dst_ref=mrec.at[slot], send_sem=meta_send.at[s], recv_sem=meta_recv.at[slot],
+            device_id=at_seq(s), device_id_type=MESH,
+        )
+
     for off in range(1, SEQ):
+        inform(lax.rem(me + off, SEQ), me).start()
         route(lax.rem(me + off, SEQ), me).start()
     query_halo = pltpu.make_async_remote_copy(
         src_ref=q_hbm.at[0, pl.ds(496, 16)], dst_ref=qs.at[pl.ds(0, 16)],
@@ -152,10 +175,12 @@
     )
     query_halo.start()
     rbuf[me] = sbuf[me]
+    mrec[me] = mbuf[me]
     for off in range(1, SEQ):
         s = lax.rem(me + SEQ - off, SEQ)
+        inform(s, s).wait_recv()
         route(s, s).wait_recv()
-    unpack_rows(rbuf, me, piece)
+    unpack_rows(rbuf, mrec, me, piece)
 
     prev_halo = pltpu.make_async_remote_copy(
         src_ref=piece.at[pl.ds(64, 16)], dst_ref=prev,
@@ -200,25 +225,30 @@
     for load in loads:
         load.wait()
     query_halo.wait_recv()
-    for i, c in enumerate(ORDER):
+
+    def step(i, carry):
+        c = jnp.where(i < 2, 1 - i, i)
         across(c, 1 - core).wait_recv()
 
-        def step(n, carry, c=c):
-            attend(c, n, me, gath, wk, wv, qs, outs)
-            return carry
-
-        lax.fori_loop(0, 4, step, 0)
-        if i + 1 < CHUNKS:
-            pass_on(ORDER[i + 1])
-        lax.fori_loop(4, 8, step, 0)
-        if c == 0:
+        @pl.when(i + 1 < CHUNKS)
+        def _():
+            pass_on(jnp.where(i < 1, 0, i + 1))
+
+        attend(c, gath, wk, wv, qs, outs)
+
+        @pl.when(c == 0)
+        def _():
             ctx_halo.start()
 
+        return carry
+
+    lax.fori_loop(0, CHUNKS, step, 0)
     ctx_halo.wait_recv()
     outs[512:528] = jnp.where(iota((16, 2048), 0) == 15, back[...], outs[512:528])
     store = pltpu.make_async_copy(outs.at[pl.ds(16, 512)], out_hbm.at[0], load_sem.at[3])
     store.start()
     for off in range(1, SEQ):
+        inform(lax.rem(me + off, SEQ), me).wait_send()
         route(lax.rem(me + off, SEQ), me).wait_send()
     query_halo.wait_send()
     prev_halo.wait_send()
@@ -231,17 +261,19 @@
 
 
 def on_device(queries, key_weight, value_weight, enc_gain, neighbour_states, slot_dest):
+    place = pl.BlockSpec(memory_space=pl.ANY)
     whole = pl.BlockSpec(memory_space=pltpu.VMEM)
-    place = pl.BlockSpec(memory_space=pl.ANY)
     dma = pltpu.SemaphoreType.DMA
-    return pl.pallas_call(
+    context = pl.pallas_call(
         kernel,
         out_shape=jax.ShapeDtypeStruct(queries.shape, BF),
         in_specs=[place, place, place, whole, whole, whole],
         out_specs=place,
         scratch_shapes=[
-            pltpu.VMEM((SEQ, 16, 640), BF),
-            pltpu.VMEM((SEQ, 16, 640), BF),
+            pltpu.VMEM((SEQ, 16, 512), BF),
+            pltpu.VMEM((SEQ, 16, 512), BF),
+            pltpu.VMEM((SEQ, 1, 128), jnp.int32),
+            pltpu.VMEM((SEQ, 1, 128), jnp.int32),
             pltpu.VMEM((80, 1024), BF),
             pltpu.VMEM((16, 1024), BF),
             pltpu.VMEM((CHUNKS, 2, CHIPS, 16, 1024), BF),
@@ -253,6 +285,8 @@
             dma((4,)),
             dma((SEQ,)),
             dma((SEQ,)),
+            dma((SEQ,)),
+            dma((SEQ,)),
             dma((3,)),
             dma((3,)),
             dma((CHUNKS, CHIPS)),
@@ -261,11 +295,13 @@
             dma((CHUNKS,)),
         ],
         compiler_params=pltpu.CompilerParams(
-            collective_id=0, has_side_effects=True, vmem_limit_bytes=44 * 1024 * 1024
+            collective_id=0, has_side_effects=True, vmem_limit_bytes=51 * 1024 * 1024
         ),
     )(
         queries, key_weight, value_weight, enc_gain.reshape(1, -1), neighbour_states, slot_dest.reshape(1, -1),
     )
+    silent = (iota(context.shape, 1) < SEGLEN - 1) & (lax.axis_index("seq") == 0)
+    return jnp.where(silent, jnp.zeros_like(context), context)
 
 
 def solution(mesh):

time: 69.4 us -> 47.4 us (0.68); the launches traced: 68.2 us -> 47.2 us
  Pallas kernels: 60.8 us -> 43.4 us
  local copies, waits for them, and re-layouts: 7.39 us -> 2.29 us
  other arithmetic: 0 us -> 1.54 us
    pallas_call x1, Pallas kernels: 60.8 us -> 43.4 us  [on_device(): pl.pallas_call(kernel, out_shape=jax.ShapeDtypeStruct(queries.shape, BF),...]
    unnamed x11 -> x6, local copies, waits for them, and re-layouts: 7.39 us -> 2.29 us
    select_n x0 -> x1, other arithmetic: none -> 1.53 us  [on_device(): return jnp.where(silent, jnp.zeros_like(context), context)]
where the time goes in v2:
time: 47.4 us; the launch traced here: 47.2 us
  Pallas kernels  43.4 us (92%)
  local copies, waits for them, and re-layouts  2.29 us (5%)
  other arithmetic  1.54 us (3%)
    pallas_call x1, Pallas kernels, on_device(): pl.pallas_call(kernel, out_shape=jax.ShapeDtypeStruct(queries.shape, BF),...  43.4 us
    unnamed x6, local copies, waits for them, and re-layouts  2.29 us
    select_n x1, other arithmetic, on_device(): return jnp.where(silent, jnp.zeros_like(context), context)  1.53 us

profile of v2, /device:TPU:1, one launch (start us, length us, event | category | flops | bytes accessed | tf_op | source)
XLA Modules:
  0.0 47.2 jit_solution(7575127463119825195)
XLA Ops:
  0.0 0.0 copy-start
  0.0 0.9 %copy-done = bf16[32,4,1024]{2,1,0:T(4,128)(2,1)S(1)} copy-done((bf16[32,4,1024]{2,1,0:T(4,128)(2,1)S(1)}, bf16[32,4,1024]{2,1,0:T(4,128)(2,1)}, u32[]{:S(2)}) %copy-start) | copy-done | bytes 262168
  1.0 0.0 copy-start.1
  1.0 0.7 %copy-done.1 = f32[1024]{0:T(1024)S(1)} copy-done((f32[1024]{0:T(1024)S(1)}, f32[1024]{0:T(1024)}, u32[]{:S(2)}) %copy-start.1) | copy-done | bytes 4120
  1.6 0.0 copy-start.2
  1.6 0.7 %copy-done.2 = s32[32]{0:T(128)S(1)} copy-done((s32[32]{0:T(128)S(1)}, s32[32]{0:T(128)}, u32[]{:S(2)}) %copy-start.2) | copy-done | bytes 152
  2.3 43.4 %shard_map.64 = bf16[1,512,2048]{2,1,0:T(8,128)(2,1)S(1)} custom-call(bf16[1,512,2048]{2,1,0:T(8,128)(2,1)} %q_hbm.1, bf16[1,1024,2048]{2,1,0:T(8,128)(2,1)} %wk_hbm.1, bf16[1,1024,2048]{2,1,0:T(8,128)(2,1)} %wv_hbm.1, f32[1,1024]{1,0:T(1,128)S(1)} %bitcast.2, bf16[32,4,1024]{2,1,0:T(4,128)(2,1)S(1)} %copy-done, s32[1,32]{1,0:T(1,128)S(1)} %bitcast.3), custom_call_target="tpu_custom_call" | custom-call | tf_op jit(solution)/shard_map/pallas_call | solution.py:267
  45.7 1.5 %broadcast_select_fusion = bf16[1,512,2048]{2,1,0:T(8,128)(2,1)} fusion(bf16[1,512,2048]{2,1,0:T(8,128)(2,1)S(1)} %shard_map.64, pred[512]{0:T(512)(128)(4,1)S(1)} %fusion), kind=kLoop, calls=%fused_computation | loop fusion | flops 1048576 | bytes 4194816 | tf_op jit(solution)/shard_map/jit(_where)/select_n | solution.py:304
  (1 shorter events, 0.0 us)
Async XLA Ops:
  0.0 0.9 %copy-start = (bf16[32,4,1024]{2,1,0:T(4,128)(2,1)S(1)}, bf16[32,4,1024]{2,1,0:T(4,128)(2,1)}, u32[]{:S(2)}) copy-start(bf16[32,4,1024]{2,1,0:T(4,128)(2,1)} %states_ref.1) | copy-start | bytes 786436
  1.0 0.7 %copy-start.1 = (f32[1024]{0:T(1024)S(1)}, f32[1024]{0:T(1024)}, u32[]{:S(2)}) copy-start(f32[1024]{0:T(1024)} %param.9) | copy-start | bytes 12292
  1.6 0.7 %copy-start.2 = (s32[32]{0:T(128)S(1)}, s32[32]{0:T(128)}, u32[]{:S(2)}) copy-start(s32[32]{0:T(128)} %param.11) | copy-start | bytes 388

commit v3 on v2

--- a/solution.py
+++ b/solution.py
@@ -14,7 +14,7 @@
 SEQ = 16
 CHIPS = 8
 CHUNKS = 4
-ORDER = (1, 0, 2, 3)
+ORDER = (1, 2, 0, 3)
 EXP2_SCALE = HD ** (-0.5) * 1.4426950408889634
 
 
@@ -70,7 +70,7 @@
     return [four[:, w].reshape(128, rows.shape[1]).astype(BF) for w in range(2)]
 
 
-def attend(c, gath, wk, wv, qs, outs):
+def attend(c, gath, wk, wv, qs, outs, tails):
     near = gath[c].reshape(256, 1024)
     last = iota((16, 256), 0) == 15
     zero = jnp.zeros((SEGLEN, HD), BF)
@@ -108,9 +108,14 @@
             two = context[128 * w : 128 * w + 128]
             both = jnp.concatenate([two[:SEGLEN, :HD], two[SEGLEN:, HD:]], axis=1)
             both = both.astype(BF)
-            outs[pl.ds(at[w] + 16, 48), cols[n]] = both[:48]
-            outs[pl.ds(at[w], 16), cols[n]] = jnp.where(last, both[48:], outs[pl.ds(at[w], 16), cols[n]])
-            outs[pl.ds(at[w] + 64, 16), cols[n]] = jnp.where(last, outs[pl.ds(at[w] + 64, 16), cols[n]], both[48:])
+            outs[pl.ds(at[w], 48), cols[n]] = both[:48]
+            tail = pl.ds(at[w] + 48, 16)
+            outs[tail, cols[n]] = jnp.where(last, outs[tail, cols[n]], both[48:])
+            if w == 0:
+                tails[c, :, cols[n]] = both[48:]
+            else:
+                tail = pl.ds(at[w] - 16, 16)
+                outs[tail, cols[n]] = jnp.where(last, both[48:], outs[tail, cols[n]])
 
     keys = [project(wk, n) for n in pairs]
     scores = [score(n, keys[n]) for n in pairs]
@@ -120,8 +125,8 @@
 
 
 def kernel(
-    q_hbm, wk_hbm, wv_hbm, gain_ref, states_ref, dest_ref, out_hbm,
-    sbuf, rbuf, mbuf, mrec, piece, prev, gath, wk, wv, qs, outs, back,
+    q_hbm, wk_hbm, wv_hbm, gain_ref, states_ref, dest_ref, outs,
+    sbuf, rbuf, mbuf, mrec, piece, prev, gath, wk, wv, qs, tails, slim, back,
     load_sem, route_send, route_recv, meta_send, meta_recv, halo_send, halo_recv, gath_send, gath_recv, pair_send, pair_recv,
 ):
     phase, me, mp = lax.axis_index("phase"), lax.axis_index("seq"), lax.axis_index("mp")
@@ -151,7 +156,6 @@
     for load in loads:
         load.start()
     pack_rows(states_ref, gain_ref, dest_ref, sbuf, mbuf)
-    outs[0:16] = jnp.zeros((16, 2048), BF)
     pl.semaphore_wait(barrier, SEQ - 1 + CHIPS - 1 + 1)
 
     def route(s, slot):
@@ -201,15 +205,19 @@
             device_id=partner, device_id_type=MESH,
         )
 
-    for c in ORDER:
-        if c == 0:
+    def send_own(c):
+        @pl.when(c == 0)
+        def _():
             prev_halo.wait_recv()
-            mine = jnp.where(iota((16, 1024), 0) < 8, prev[...], piece[0:16])
-        else:
-            mine = piece[16 * c : 16 * c + 16]
-        gath[c, core, chip] = mine
+
+        mine = piece[pl.ds(pl.multiple_of(16 * c, 16), 16), :]
+        gath[c, core, chip] = jnp.where((iota((16, 1024), 0) < 8) & (c == 0), prev[...], mine)
         for off in range(1, CHIPS):
             give(c, lax.rem(chip + off, CHIPS), chip).start()
+
+    def sent(c):
+        for off in range(1, CHIPS):
+            give(c, lax.rem(chip + off, CHIPS), chip).wait_send()
 
     def pass_on(c):
         for off in range(1, CHIPS):
@@ -218,46 +226,66 @@
         across(c, core).start()
 
     ctx_halo = pltpu.make_async_remote_copy(
-        src_ref=outs.at[pl.ds(0, 16)], dst_ref=back,
+        src_ref=slim, dst_ref=back,
         send_sem=halo_send.at[2], recv_sem=halo_recv.at[2], device_id=at_seq(ahead), device_id_type=MESH,
     )
+    send_own(jnp.int32(ORDER[0]))
+    send_own(jnp.int32(ORDER[1]))
     pass_on(ORDER[0])
+    send_own(jnp.int32(ORDER[2]))
+    send_own(jnp.int32(ORDER[3]))
     for load in loads:
         load.wait()
     query_halo.wait_recv()
 
+    def nth(i):
+        return sum(jnp.where(i == j, c, 0) for j, c in enumerate(ORDER))
+
     def step(i, carry):
-        c = jnp.where(i < 2, 1 - i, i)
-        across(c, 1 - core).wait_recv()
+        c = nth(i)
 
         @pl.when(i + 1 < CHUNKS)
         def _():
-            pass_on(jnp.where(i < 1, 0, i + 1))
-
-        attend(c, gath, wk, wv, qs, outs)
+            pass_on(nth(i + 1))
+
+        across(c, 1 - core).wait_recv()
+        attend(c, gath, wk, wv, qs, outs, tails)
 
         @pl.when(c == 0)
         def _():
+            rows = jnp.zeros((16, HD), F32)
+            for h in range(16):
+                row = tails[0, :, HD * h : HD * h + HD].astype(F32)[15:16]
+                rows = jnp.where(iota((16, HD), 0) == h, jnp.broadcast_to(row, (16, HD)), rows)
+            slim[...] = rows.astype(BF)
             ctx_halo.start()
+
+        @pl.when(c > 0)
+        def _():
+            tail = pl.ds(pl.multiple_of(2 * SEGLEN * c - 16, 16), 16)
+            outs[tail, :] = jnp.where(iota((16, 2048), 0) == 15, tails[c], outs[tail, :])
 
         return carry
 
     lax.fori_loop(0, CHUNKS, step, 0)
     ctx_halo.wait_recv()
-    outs[512:528] = jnp.where(iota((16, 2048), 0) == 15, back[...], outs[512:528])
-    store = pltpu.make_async_copy(outs.at[pl.ds(16, 512)], out_hbm.at[0], load_sem.at[3])
-    store.start()
+    back_rows = back[...].astype(F32)
+    for h in range(16):
+        col = slice(HD * h, HD * h + HD)
+        row = jnp.broadcast_to(back_rows[h : h + 1], (16, HD)).astype(BF)
+        outs[496:512, col] = jnp.where(iota((16, HD), 0) == 15, row, outs[496:512, col])
     for off in range(1, SEQ):
         inform(lax.rem(me + off, SEQ), me).wait_send()
         route(lax.rem(me + off, SEQ), me).wait_send()
     query_halo.wait_send()
     prev_halo.wait_send()
     ctx_halo.wait_send()
+    sent(ORDER[0])
+    sent(ORDER[1])
+    sent(ORDER[2])
+    sent(ORDER[3])
     for c in ORDER:
-        for off in range(1, CHIPS):
-            give(c, lax.rem(chip + off, CHIPS), chip).wait_send()
         across(c, core).wait_send()
-    store.wait()
 
 
 def on_device(queries, key_weight, value_weight, enc_gain, neighbour_states, slot_dest):
@@ -266,9 +294,9 @@
     dma = pltpu.SemaphoreType.DMA
     context = pl.pallas_call(
         kernel,
-        out_shape=jax.ShapeDtypeStruct(queries.shape, BF),
+        out_shape=jax.ShapeDtypeStruct((512, 2048), BF),
         in_specs=[place, place, place, whole, whole, whole],
-        out_specs=place,
+        out_specs=whole,
         scratch_shapes=[
             pltpu.VMEM((SEQ, 16, 512), BF),
             pltpu.VMEM((SEQ, 16, 512), BF),
@@ -280,9 +308,10 @@
             pltpu.VMEM((1024, 2048), BF),
             pltpu.VMEM((1024, 2048), BF),
             pltpu.VMEM((528, 2048), BF),
-            pltpu.VMEM((528, 2048), BF),
-            pltpu.VMEM((16, 2048), BF),
-            dma((4,)),
+            pltpu.VMEM((CHUNKS, 16, 2048), BF),
+            pltpu.VMEM((16, HD), BF),
+            pltpu.VMEM((16, HD), BF),
+            dma((3,)),
             dma((SEQ,)),
             dma((SEQ,)),
             dma((SEQ,)),
@@ -295,11 +324,12 @@
             dma((CHUNKS,)),
         ],
         compiler_params=pltpu.CompilerParams(
-            collective_id=0, has_side_effects=True, vmem_limit_bytes=51 * 1024 * 1024
+            collective_id=0, has_side_effects=True, vmem_limit_bytes=52000 * 1024
         ),
     )(
         queries, key_weight, value_weight, enc_gain.reshape(1, -1), neighbour_states, slot_dest.reshape(1, -1),
     )
+    context = context[None]
     silent = (iota(context.shape, 1) < SEGLEN - 1) & (lax.axis_index("seq") == 0)
     return jnp.where(silent, jnp.zeros_like(context), context)
 

time: 47.4 us -> 45.8 us (0.966)
  Pallas kernels: 43.4 us -> 41.5 us
    pallas_call x1, Pallas kernels: 43.4 us -> 41.5 us  [on_device(): pl.pallas_call(kernel, out_shape=jax.ShapeDtypeStruct((512, 2048), BF), i...]
where the time goes in v3:
time: 45.8 us; the launch traced here: 45.3 us
  Pallas kernels  41.5 us (91%)
  local copies, waits for them, and re-layouts  2.29 us (5%)
  other arithmetic  1.54 us (3%)
    pallas_call x1, Pallas kernels, on_device(): pl.pallas_call(kernel, out_shape=jax.ShapeDtypeStruct((512, 2048), BF), i...  41.5 us
    unnamed x6, local copies, waits for them, and re-layouts  2.29 us
    select_n x1, other arithmetic, on_device(): return jnp.where(silent, jnp.zeros_like(context), context)  1.53 us

profile of v3, /device:TPU:1, one launch (start us, length us, event | category | flops | bytes accessed | tf_op | source)
XLA Modules:
  0.0 45.3 jit_solution(8941044550811546743)
XLA Ops:
  0.0 0.0 copy-start
  0.0 0.9 %copy-done = bf16[32,4,1024]{2,1,0:T(4,128)(2,1)S(1)} copy-done((bf16[32,4,1024]{2,1,0:T(4,128)(2,1)S(1)}, bf16[32,4,1024]{2,1,0:T(4,128)(2,1)}, u32[]{:S(2)}) %copy-start) | copy-done | bytes 262168
  1.0 0.0 copy-start.1
  1.0 0.7 %copy-done.1 = f32[1024]{0:T(1024)S(1)} copy-done((f32[1024]{0:T(1024)S(1)}, f32[1024]{0:T(1024)}, u32[]{:S(2)}) %copy-start.1) | copy-done | bytes 4120
  1.6 0.0 copy-start.2
  1.6 0.7 %copy-done.2 = s32[32]{0:T(128)S(1)} copy-done((s32[32]{0:T(128)S(1)}, s32[32]{0:T(128)}, u32[]{:S(2)}) %copy-start.2) | copy-done | bytes 152
  2.3 41.5 %shard_map.64 = bf16[512,2048]{1,0:T(8,128)(2,1)S(1)} custom-call(bf16[1,512,2048]{2,1,0:T(8,128)(2,1)} %q_hbm.1, bf16[1,1024,2048]{2,1,0:T(8,128)(2,1)} %wk_hbm.1, bf16[1,1024,2048]{2,1,0:T(8,128)(2,1)} %wv_hbm.1, f32[1,1024]{1,0:T(1,128)S(1)} %bitcast.4, bf16[32,4,1024]{2,1,0:T(4,128)(2,1)S(1)} %copy-done, s32[1,32]{1,0:T(1,128)S(1)} %bitcast.5), custom_call_target="tpu_custom_call" | custom-call | tf_op jit(solution)/shard_map/pallas_call | solution.py:295
  43.8 1.5 %select_bitcast_fusion = bf16[1,512,2048]{2,1,0:T(8,128)(2,1)} fusion(bf16[512,2048]{1,0:T(8,128)(2,1)S(1)} %shard_map.64, pred[512]{0:T(512)(128)(4,1)S(1)} %fusion), kind=kLoop, calls=%fused_computation | loop fusion | flops 1048576 | bytes 4194816 | tf_op jit(solution)/shard_map/jit(_where)/select_n | solution.py:334
  (1 shorter events, 0.0 us)
Async XLA Ops:
  0.0 0.9 %copy-start = (bf16[32,4,1024]{2,1,0:T(4,128)(2,1)S(1)}, bf16[32,4,1024]{2,1,0:T(4,128)(2,1)}, u32[]{:S(2)}) copy-start(bf16[32,4,1024]{2,1,0:T(4,128)(2,1)} %states_ref.1) | copy-start | bytes 786436
  1.0 0.7 %copy-start.1 = (f32[1024]{0:T(1024)S(1)}, f32[1024]{0:T(1024)}, u32[]{:S(2)}) copy-start(f32[1024]{0:T(1024)} %param.9) | copy-start | bytes 12292
  1.6 0.7 %copy-start.2 = (s32[32]{0:T(128)S(1)}, s32[32]{0:T(128)}, u32[]{:S(2)}) copy-start(s32[32]{0:T(128)} %param.11) | copy-start | bytes 388

commit v4 on v3

--- a/solution.py
+++ b/solution.py
@@ -124,9 +124,17 @@
         finish(n, scores[n], vals[n])
 
 
+def last_row_by_head(tile):
+    rows = jnp.zeros((16, HD), F32)
+    for h in range(16):
+        row = tile[:, HD * h : HD * h + HD].astype(F32)[15:16]
+        rows = jnp.where(iota((16, HD), 0) == h, jnp.broadcast_to(row, (16, HD)), rows)
+    return rows.astype(BF)
+
+
 def kernel(
     q_hbm, wk_hbm, wv_hbm, gain_ref, states_ref, dest_ref, outs,
-    sbuf, rbuf, mbuf, mrec, piece, prev, gath, wk, wv, qs, tails, slim, back,
+    sbuf, rbuf, mbuf, mrec, piece, prev, gath, wk, wv, qs, edge, tails, slim, back,
     load_sem, route_send, route_recv, meta_send, meta_recv, halo_send, halo_recv, gath_send, gath_recv, pair_send, pair_recv,
 ):
     phase, me, mp = lax.axis_index("phase"), lax.axis_index("seq"), lax.axis_index("mp")
@@ -148,6 +156,8 @@
         pl.semaphore_signal(barrier, inc=1, device_id=at_chip(lax.rem(chip + off, CHIPS)), device_id_type=MESH)
     pl.semaphore_signal(barrier, inc=1, device_id=partner, device_id_type=MESH)
 
+    edge_load = pltpu.make_async_copy(q_hbm.at[0, pl.ds(496, 16)], edge, load_sem.at[3])
+    edge_load.start()
     loads = [
         pltpu.make_async_copy(q_hbm.at[0], qs.at[pl.ds(16, 512)], load_sem.at[0]),
         pltpu.make_async_copy(wk_hbm.at[0], wk, load_sem.at[1]),
@@ -156,6 +166,8 @@
     for load in loads:
         load.start()
     pack_rows(states_ref, gain_ref, dest_ref, sbuf, mbuf)
+    edge_load.wait()
+    slim[0] = last_row_by_head(edge[...])
     pl.semaphore_wait(barrier, SEQ - 1 + CHIPS - 1 + 1)
 
     def route(s, slot):
@@ -174,7 +186,7 @@
         inform(lax.rem(me + off, SEQ), me).start()
         route(lax.rem(me + off, SEQ), me).start()
     query_halo = pltpu.make_async_remote_copy(
-        src_ref=q_hbm.at[0, pl.ds(496, 16)], dst_ref=qs.at[pl.ds(0, 16)],
+        src_ref=slim.at[0], dst_ref=back.at[0],
         send_sem=halo_send.at[0], recv_sem=halo_recv.at[0], device_id=at_seq(after), device_id_type=MESH,
     )
     query_halo.start()
@@ -226,7 +238,7 @@
         across(c, core).start()
 
     ctx_halo = pltpu.make_async_remote_copy(
-        src_ref=slim, dst_ref=back,
+        src_ref=slim.at[1], dst_ref=back.at[1],
         send_sem=halo_send.at[2], recv_sem=halo_recv.at[2], device_id=at_seq(ahead), device_id_type=MESH,
     )
     send_own(jnp.int32(ORDER[0]))
@@ -237,6 +249,10 @@
     for load in loads:
         load.wait()
     query_halo.wait_recv()
+    query_rows = back[0].astype(F32)
+    for h in range(16):
+        row = jnp.broadcast_to(query_rows[h : h + 1], (16, HD))
+        qs[0:16, HD * h : HD * h + HD] = row.astype(BF)
 
     def nth(i):
         return sum(jnp.where(i == j, c, 0) for j, c in enumerate(ORDER))
@@ -253,11 +269,7 @@
 
         @pl.when(c == 0)
         def _():
-            rows = jnp.zeros((16, HD), F32)
-            for h in range(16):
-                row = tails[0, :, HD * h : HD * h + HD].astype(F32)[15:16]
-                rows = jnp.where(iota((16, HD), 0) == h, jnp.broadcast_to(row, (16, HD)), rows)
-            slim[...] = rows.astype(BF)
+            slim[1] = last_row_by_head(tails[0])
             ctx_halo.start()
 
         @pl.when(c > 0)
@@ -269,7 +281,7 @@
 
     lax.fori_loop(0, CHUNKS, step, 0)
     ctx_halo.wait_recv()
-    back_rows = back[...].astype(F32)
+    back_rows = back[1].astype(F32)
     for h in range(16):
         col = slice(HD * h, HD * h + HD)
         row = jnp.broadcast_to(back_rows[h : h + 1], (16, HD)).astype(BF)
@@ -308,10 +320,11 @@
             pltpu.VMEM((1024, 2048), BF),
             pltpu.VMEM((1024, 2048), BF),
             pltpu.VMEM((528, 2048), BF),
+            pltpu.VMEM((16, 2048), BF),
             pltpu.VMEM((CHUNKS, 16, 2048), BF),
-            pltpu.VMEM((16, HD), BF),
-            pltpu.VMEM((16, HD), BF),
-            dma((3,)),
+            pltpu.VMEM((2, 16, HD), BF),
+            pltpu.VMEM((2, 16, HD), BF),
+            dma((4,)),
             dma((SEQ,)),
             dma((SEQ,)),
             dma((SEQ,)),

time: 45.8 us -> 45.6 us (level)
  no operation moved by 1% of the time
where the time goes in v4:
time: 45.6 us; the launch traced here: 45.5 us
  Pallas kernels  41.6 us (91%)
  local copies, waits for them, and re-layouts  2.29 us (5%)
  other arithmetic  1.54 us (3%)
    pallas_call x1, Pallas kernels, on_device(): pl.pallas_call(kernel, out_shape=jax.ShapeDtypeStruct((512, 2048), BF), i...  41.6 us
    unnamed x6, local copies, waits for them, and re-layouts  2.29 us
    select_n x1, other arithmetic, on_device(): return jnp.where(silent, jnp.zeros_like(context), context)  1.53 us

profile of v4, /device:TPU:1, one launch (start us, length us, event | category | flops | bytes accessed | tf_op | source)
XLA Modules:
  0.0 45.5 jit_solution(16644360207044038369)
XLA Ops:
  0.0 0.0 copy-start
  0.0 0.9 %copy-done = bf16[32,4,1024]{2,1,0:T(4,128)(2,1)S(1)} copy-done((bf16[32,4,1024]{2,1,0:T(4,128)(2,1)S(1)}, bf16[32,4,1024]{2,1,0:T(4,128)(2,1)}, u32[]{:S(2)}) %copy-start) | copy-done | bytes 262168
  1.0 0.0 copy-start.1
  1.0 0.7 %copy-done.1 = f32[1024]{0:T(1024)S(1)} copy-done((f32[1024]{0:T(1024)S(1)}, f32[1024]{0:T(1024)}, u32[]{:S(2)}) %copy-start.1) | copy-done | bytes 4120
  1.6 0.0 copy-start.2
  1.6 0.7 %copy-done.2 = s32[32]{0:T(128)S(1)} copy-done((s32[32]{0:T(128)S(1)}, s32[32]{0:T(128)}, u32[]{:S(2)}) %copy-start.2) | copy-done | bytes 152
  2.3 41.6 %shard_map.64 = bf16[512,2048]{1,0:T(8,128)(2,1)S(1)} custom-call(bf16[1,512,2048]{2,1,0:T(8,128)(2,1)} %q_hbm.1, bf16[1,1024,2048]{2,1,0:T(8,128)(2,1)} %wk_hbm.1, bf16[1,1024,2048]{2,1,0:T(8,128)(2,1)} %wv_hbm.1, f32[1,1024]{1,0:T(1,128)S(1)} %bitcast.4, bf16[32,4,1024]{2,1,0:T(4,128)(2,1)S(1)} %copy-done, s32[1,32]{1,0:T(1,128)S(1)} %bitcast.5), custom_call_target="tpu_custom_call" | custom-call | tf_op jit(solution)/shard_map/pallas_call | solution.py:307
  43.9 1.5 %select_bitcast_fusion = bf16[1,512,2048]{2,1,0:T(8,128)(2,1)} fusion(bf16[512,2048]{1,0:T(8,128)(2,1)S(1)} %shard_map.64, pred[512]{0:T(512)(128)(4,1)S(1)} %fusion), kind=kLoop, calls=%fused_computation | loop fusion | flops 1048576 | bytes 4194816 | tf_op jit(solution)/shard_map/jit(_where)/select_n | solution.py:347
  (1 shorter events, 0.0 us)
Async XLA Ops:
  0.0 0.9 %copy-start = (bf16[32,4,1024]{2,1,0:T(4,128)(2,1)S(1)}, bf16[32,4,1024]{2,1,0:T(4,128)(2,1)}, u32[]{:S(2)}) copy-start(bf16[32,4,1024]{2,1,0:T(4,128)(2,1)} %states_ref.1) | copy-start | bytes 786436
  1.0 0.7 %copy-start.1 = (f32[1024]{0:T(1024)S(1)}, f32[1024]{0:T(1024)}, u32[]{:S(2)}) copy-start(f32[1024]{0:T(1024)} %param.9) | copy-start | bytes 12292
  1.6 0.7 %copy-start.2 = (s32[32]{0:T(128)S(1)}, s32[32]{0:T(128)}, u32[]{:S(2)}) copy-start(s32[32]{0:T(128)} %param.11) | copy-start | bytes 388

commit v5 on v4

--- a/solution.py
+++ b/solution.py
@@ -286,6 +286,12 @@
         col = slice(HD * h, HD * h + HD)
         row = jnp.broadcast_to(back_rows[h : h + 1], (16, HD)).astype(BF)
         outs[496:512, col] = jnp.where(iota((16, HD), 0) == 15, row, outs[496:512, col])
+
+    @pl.when(me == 0)
+    def _():
+        outs[0:48, :] = jnp.zeros((48, 2048), BF)
+        outs[48:64, :] = jnp.where(iota((16, 2048), 0) == 15, outs[48:64, :], jnp.zeros((16, 2048), BF))
+
     for off in range(1, SEQ):
         inform(lax.rem(me + off, SEQ), me).wait_send()
         route(lax.rem(me + off, SEQ), me).wait_send()
@@ -343,8 +349,7 @@
         queries, key_weight, value_weight, enc_gain.reshape(1, -1), neighbour_states, slot_dest.reshape(1, -1),
     )
     context = context[None]
-    silent = (iota(context.shape, 1) < SEGLEN - 1) & (lax.axis_index("seq") == 0)
-    return jnp.where(silent, jnp.zeros_like(context), context)
+    return context
 
 
 def solution(mesh):

time: 45.6 us -> 45.4 us (level)
  other arithmetic: 1.54 us -> 0 us
  local copies, waits for them, and re-layouts: 2.29 us -> 3.61 us
    select_n x1 -> x0, other arithmetic: 1.53 us -> none  [on_device(): return jnp.where(silent, jnp.zeros_like(context), context)]
    unnamed x6 -> x7, local copies, waits for them, and re-layouts: 2.29 us -> 3.61 us
where the time goes in v5:
time: 45.4 us; the launch traced here: 45.3 us
  Pallas kernels  41.7 us (92%)
  local copies, waits for them, and re-layouts  3.61 us (8%)
    pallas_call x1, Pallas kernels, on_device(): pl.pallas_call(kernel, out_shape=jax.ShapeDtypeStruct((512, 2048), BF), i...  41.7 us
    unnamed x7, local copies, waits for them, and re-layouts  3.61 us

profile of v5, /device:TPU:1, one launch (start us, length us, event | category | flops | bytes accessed | tf_op | source)
XLA Modules:
  0.0 45.3 jit_solution(35527691904209568)
XLA Ops:
  0.0 0.0 copy-start
  0.0 0.9 %copy-done = bf16[32,4,1024]{2,1,0:T(4,128)(2,1)S(1)} copy-done((bf16[32,4,1024]{2,1,0:T(4,128)(2,1)S(1)}, bf16[32,4,1024]{2,1,0:T(4,128)(2,1)}, u32[]{:S(2)}) %copy-start) | copy-done | bytes 262168
  1.0 0.0 copy-start.1
  1.0 0.7 %copy-done.1 = f32[1024]{0:T(1024)S(1)} copy-done((f32[1024]{0:T(1024)S(1)}, f32[1024]{0:T(1024)}, u32[]{:S(2)}) %copy-start.1) | copy-done | bytes 4120
  1.6 0.0 copy-start.2
  1.6 0.7 %copy-done.2 = s32[32]{0:T(128)S(1)} copy-done((s32[32]{0:T(128)S(1)}, s32[32]{0:T(128)}, u32[]{:S(2)}) %copy-start.2) | copy-done | bytes 152
  2.3 41.7 %shard_map.64 = bf16[512,2048]{1,0:T(8,128)(2,1)S(1)} custom-call(bf16[1,512,2048]{2,1,0:T(8,128)(2,1)} %q_hbm.1, bf16[1,1024,2048]{2,1,0:T(8,128)(2,1)} %wk_hbm.1, bf16[1,1024,2048]{2,1,0:T(8,128)(2,1)} %wv_hbm.1, f32[1,1024]{1,0:T(1,128)S(1)} %bitcast.4, bf16[32,4,1024]{2,1,0:T(4,128)(2,1)S(1)} %copy-done, s32[1,32]{1,0:T(1,128)S(1)} %bitcast.5), custom_call_target="tpu_custom_call" | custom-call | tf_op jit(solution)/shard_map/pallas_call | solution.py:313
  44.0 1.3 %copy.8 = bf16[1,512,2048]{2,1,0:T(8,128)(2,1)} copy(bf16[1,512,2048]{2,1,0:T(8,128)(2,1)S(1)} %bitcast.3) | data formatting | bytes 4194304
Async XLA Ops:
  0.0 0.9 %copy-start = (bf16[32,4,1024]{2,1,0:T(4,128)(2,1)S(1)}, bf16[32,4,1024]{2,1,0:T(4,128)(2,1)}, u32[]{:S(2)}) copy-start(bf16[32,4,1024]{2,1,0:T(4,128)(2,1)} %states_ref.1) | copy-start | bytes 786436
  1.0 0.7 %copy-start.1 = (f32[1024]{0:T(1024)S(1)}, f32[1024]{0:T(1024)}, u32[]{:S(2)}) copy-start(f32[1024]{0:T(1024)} %param.9) | copy-start | bytes 12292
  1.6 0.7 %copy-start.2 = (s32[32]{0:T(128)S(1)}, s32[32]{0:T(128)}, u32[]{:S(2)}) copy-start(s32[32]{0:T(128)} %param.11) | copy-start | bytes 388
